TPU v7x, 128 devices: a whole 4x4x4 slice. The times are simulated.
128 devices in a mesh: hi: 16 (over z, x), lo: 8 (over y, core).
Axes of the slice: x: 4, y: 4, z: 4, core: 2. Of those that a mesh axis runs over, the one named last changes fastest.
Arguments:
- panel: float32 [2097152, 128], P(('hi', 'lo')), may hold values from -6 to 6
- signs: int32 [2097152], P(('hi', 'lo')), may hold values from -1 to 1, as said below
- sample_rows: int32 [8192], replicated, may hold values from 0 to 2097151, as said below
Outputs:
- q_factor: float32 [8192, 128], P(('hi', 'lo'))
- r_factor: float32 [128, 128], replicated
Inputs may be any that keep to these rules, and one draw needn't show every extreme that they name: `sample_rows`: entries 64 * d to 64 * (d + 1) - 1 are rows in d * 16384 to (d + 1) * 16384 - 1, drawn evenly with replacement; the value 0 and the value 2097152 - 1 occur in every draw. `signs`: every entry is -1 or 1.
All inputs are finite; a program needn't handle non-finite values.
Results may differ from a plain program's by a relative error of at most 0.000076.
Values sent between devices are 32-bit elements; how exact they have to be, the bound alone decides.
A program may use at most 128 MiB of HBM per device.

v0:
```python
import math

import jax
import jax.numpy as jnp
from jax import lax
from jax.sharding import PartitionSpec as P

LOCAL_A = 128


def parity_of(values, bit_total):
    parity = jnp.zeros(values.shape, jnp.int32)
    for bit_place in range(max(bit_total, 1)):
        parity = parity + jnp.bitwise_and(jnp.right_shift(values, bit_place), 1)
    return parity


def hadamard(order):
    index = jnp.arange(order, dtype=jnp.int32)
    common = jnp.bitwise_and(index[:, None], index[None, :])
    parity = parity_of(common, order.bit_length() - 1)
    return jnp.where(parity % 2 == 0, 1.0, -1.0).astype(jnp.float32)


def shards(panel, signs, sample_rows):
    highest = lax.Precision.HIGHEST
    row_count, col_count = panel.shape
    device_count = lax.axis_size(("hi", "lo"))
    total_rows = row_count * device_count
    outer_order = LOCAL_A
    inner_order = row_count // outer_order
    per_device = sample_rows.shape[0] // device_count
    position = lax.axis_index(("hi", "lo"))
    signed = panel * signs[:, None].astype(jnp.float32)
    blocks = signed.reshape(outer_order, inner_order, col_count)
    blocks = jnp.einsum("ij,jbc->ibc", hadamard(outer_order), blocks, precision=highest)
    blocks = jnp.einsum("ab,ibc->iac", hadamard(inner_order), blocks, precision=highest)
    local_pass = blocks.reshape(row_count, col_count)
    width_lo = lax.axis_size("lo")
    shuffled = lax.all_to_all(
        local_pass.reshape(1, row_count, col_count), "lo", split_axis=1, concat_axis=0, tiled=True
    )
    shuffled = jnp.einsum("ij,jrc->irc", hadamard(width_lo), shuffled, precision=highest)
    shuffled = lax.all_to_all(shuffled, "lo", split_axis=0, concat_axis=1, tiled=True)
    width_hi = lax.axis_size("hi")
    shuffled = lax.all_to_all(shuffled, "hi", split_axis=1, concat_axis=0, tiled=True)
    shuffled = jnp.einsum("ij,jrc->irc", hadamard(width_hi), shuffled, precision=highest)
    shuffled = lax.all_to_all(shuffled, "hi", split_axis=0, concat_axis=1, tiled=True)
    full_pass = shuffled.reshape(row_count, col_count)
    own_rows = (
        lax.dynamic_slice_in_dim(sample_rows, position * per_device, per_device)
        - position * row_count
    )
    sketch = jnp.take(full_pass, own_rows, axis=0) / math.sqrt(total_rows)
    partial_gram = jnp.dot(sketch.T, sketch, precision=highest, preferred_element_type=jnp.float32)
    gram = lax.psum(partial_gram, ("hi", "lo")) / (per_device * device_count)
    lower = jnp.linalg.cholesky(gram)
    q_factor = lax.linalg.triangular_solve(
        lower, sketch, left_side=False, lower=True, transpose_a=True
    )
    return (q_factor, lower.T)


def solution(mesh):
    placed = (P(("hi", "lo"), None), P(("hi", "lo")), P())
    return jax.shard_map(
        shards, mesh=mesh, in_specs=placed, out_specs=(P(("hi", "lo"), None), P()), check_vma=False
    )
```

profile of v0, /device:TPU:0, one launch (start us, length us, event | category | flops | bytes accessed | tf_op | source)
XLA Modules:
  0.0 675.8 jit_solution(12756283446450316821)
XLA Ops:
  7.2 0.8 convert_element_type.4
  8.0 8.7 %broadcast_multiply_fusion = f32[16384,128]{1,0:T(8,128)S(1)} fusion(f32[16384,128]{1,0:T(8,128)} %param.3, f32[16384]{0:T(1024)S(1)} %convert_element_type.4), kind=kLoop, calls=%fused_computation.9 | loop fusion | flops 2097152 | bytes 16842752 | tf_op jit(solution)/shard_map/mul | solution.py:34
  16.7 12.5 %fusion.6 = f32[128,128,128]{2,0,1:T(8,128)S(1)} fusion(f32[128,128,128]{2,1,0:T(8,128)S(1)} %bitcast.34), kind=kOutput, calls=%fused_computation.7 | convolution fusion | flops 3221782528 | bytes 16777216 | tf_op jit(solution)/shard_map/ij,jbc->ibc/dot_general | solution.py:36
  29.2 13.8 %fusion.4 = f32[128,128,128]{1,2,0:T(8,128)S(1)} fusion(f32[128,128,128]{2,0,1:T(8,128)S(1)} %fusion.6), kind=kOutput, calls=%fused_computation.5 | convolution fusion | flops 3221782528 | bytes 16777216 | tf_op jit(solution)/shard_map/ab,ibc->iac/dot_general | solution.py:37
  43.0 100.3 %all_to_all.45 = f32[1,16384,128]{2,0,1:T(1,128)S(1)} all-to-all(f32[1,16384,128]{2,0,1:T(1,128)S(1)} %bitcast.35), channel_id=1, replica_groups=mesh['hi'=16,'lo'=8] {'lo'}, dimensions={1} | all-to-all | bytes 16777216 | tf_op jit(solution)/shard_map/all_to_all | solution.py:40
  143.3 14.0 %fusion.2 = f32[8,2048,128]{2,0,1:T(8,128)S(1)} fusion(f32[8,2048,128]{2,1,0:T(8,128)S(1)} %bitcast.36), kind=kOutput, calls=%fused_computation.3 | convolution fusion | flops 201328000 | bytes 16777216 | tf_op jit(solution)/shard_map/ij,jrc->irc/dot_general | solution.py:43
  157.3 1.6 copy.19
  158.9 98.5 %all_to_all.46 = f32[8,2048,128]{2,1,0:T(8,128)S(1)} all-to-all(f32[8,2048,128]{2,1,0:T(8,128)S(1)} %copy.19), channel_id=1, replica_groups=mesh['hi'=16,'lo'=8] {'lo'}, dimensions={0} | all-to-all | bytes 16777216 | tf_op jit(solution)/shard_map/all_to_all | solution.py:44
  257.4 103.1 %all_to_all.47 = f32[1,16384,128]{2,0,1:T(1,128)S(1)} all-to-all(f32[1,16384,128]{2,0,1:T(1,128)S(1)} %bitcast.37), channel_id=1, replica_groups=mesh['hi'=16,'lo'=8] {'hi'}, dimensions={1} | all-to-all | bytes 16777216 | tf_op jit(solution)/shard_map/all_to_all | solution.py:46
  360.5 11.7 %fusion = f32[16,1024,128]{2,0,1:T(8,128)S(1)} fusion(f32[16,1024,128]{2,1,0:T(8,128)S(1)} %bitcast.38), kind=kOutput, calls=%fused_computation.1 | convolution fusion | flops 402659584 | bytes 16777216 | tf_op jit(solution)/shard_map/ij,jrc->irc/dot_general | solution.py:47
  372.2 5.9 copy.22
  378.2 4.7 all-to-all-start.3
  382.9 0.0 all-reduce.2.cloned.1.call-start
  383.0 0.8 compare_and_fusion
  383.7 120.9 %all-to-all-done.3 = f32[16,1024,128]{2,1,0:T(8,128)} async-done(((f32[16,1024,128]{2,1,0:T(8,128)}), f32[16,1024,128]{2,1,0:T(8,128)}, u32[]{:S(2)}, u32[]{:S(2)}) %all-to-all-start.3) | async-done | bytes 8388640 | tf_op jit(solution)/shard_map/all_to_all | solution.py:48
  504.6 4.0 gather_fusion
  508.6 1.0 fusion.24
  509.6 0.0 all-reduce.2.cloned.1.call-update
  509.6 132.9 %all-reduce.2.cloned.1.call-done = f32[128,128]{0,1:T(8,128)} async-done(((f32[128,128]{0,1:T(8,128)}), f32[128,128]{0,1:T(8,128)}) %all-reduce.2.cloned.1.call-update) | async-done | bytes 65552 | tf_op jit(solution)/shard_map/psum | solution.py:56
  642.5 0.8 broadcast_multiply_fusion.1
  643.3 0.1 copy.24
  643.4 0.9 fusion.12
  644.3 11.7 %cholesky.16 = f32[128,128]{1,0:T(8,128)S(1)} custom-call(f32[128,128]{1,0:T(8,128)S(1)} %fusion.12), custom_call_target="Cholesky" | custom-call | tf_op jit(solution)/shard_map/jit(cholesky)/cholesky | solution.py:57
  656.0 0.6 compare_reduce_fusion
  656.7 0.7 fusion.17
  657.4 9.8 %custom-call.6 = f32[1,128,128]{1,2,0:T(8,128)S(1)} custom-call(f32[1,128,128]{2,1,0:T(8,128)S(1)} %get-tuple-element.11), custom_call_target="InvertDiagBlocksLowerTriangular" | custom-call | tf_op jit(solution)/shard_map/triangular_solve | solution.py:58
  667.2 0.9 fusion.10
  668.0 0.7 copy.25
  (2 shorter events, 0.0 us)
Async XLA Ops:
  378.2 126.5 %all-to-all-start.3 = ((f32[16,1024,128]{2,1,0:T(8,128)}), f32[16,1024,128]{2,1,0:T(8,128)}, u32[]{:S(2)}, u32[]{:S(2)}) async-start(f32[16,1024,128]{2,1,0:T(8,128)} %copy.22), calls=%async_computation.3 | async-start | bytes 16777216 | tf_op jit(solution)/shard_map/all_to_all | solution.py:48
  382.9 259.6 %all-reduce.2.cloned.1.call-start = ((), (), s32[]{:S(2)}) async-start(), calls=%async_computation.4 | async-start | bytes 131072 | tf_op jit(solution)/shard_map/psum | solution.py:56
Sparse Core Ops, SparseCore 0:
  509.7 132.7 all-reduce.1
where the time goes:
time: 689 us; the launch traced here: 676 us
  blocking collectives  302 us (44%)
  waiting for transfers between devices  254 us (37%)
  matrix products  53.8 us (8%)
  other arithmetic  34.9 us (5%)
  between operations  14.3 us (2%)
  local copies, waits for them, and re-layouts  12.4 us (2%)
    psum x1, waiting for transfers between devices, shards(): gram = lax.psum(partial_gram, ('hi', 'lo')) / (per_device * device_count)  133 us
    all_to_all x1, waiting for transfers between devices, shards(): lax.all_to_all(shuffled, 'hi', split_axis=0, concat_axis=1, tiled=True)  121 us
    all_to_all x1, blocking collectives, shards(): lax.all_to_all(shuffled, 'hi', split_axis=1, concat_axis=0, tiled=True)  103 us
    all_to_all x1, blocking collectives, shards(): lax.all_to_all(local_pass.reshape(1, row_count, col_count), 'lo', split_a...  100 us
    all_to_all x1, blocking collectives, shards(): lax.all_to_all(shuffled, 'lo', split_axis=0, concat_axis=1, tiled=True)  98.5 us
    dot_general x1, matrix products, shards(): jnp.einsum('ij,jrc->irc', hadamard(width_lo), shuffled, precision=highest)  14 us
    dot_general x1, matrix products, shards(): jnp.einsum('ab,ibc->iac', hadamard(inner_order), blocks, precision=highest)  13.8 us
  transfers between devices with their start and end apart: 2, of which 2 were waited for; matrix products, arithmetic and copies ran while one was open for 0% of the time, Pallas kernels for 0%

commit v1 on v0

v1 whole, which is shorter than its diff:
```python
import functools
import math

import jax
import jax.numpy as jnp
from jax import lax
from jax.experimental import pallas as pl
from jax.experimental.pallas import tpu as pltpu
from jax.sharding import PartitionSpec as P

MESH = pl.DeviceIdType.MESH
COLS = 128
MIX = 256
LOADS = 8
BLOCK = 16
PARTS = ((0, 24), (24, 24), (48, 16))
ORDERS = ((0, 1, 2), (1, 2, 0), (2, 0, 1))
GRAM_PARTS = ((0, 48), (48, 40), (88, 40))


def parity_sign(value, bits):
    total = value & 1
    for place in range(1, bits):
        total = total + ((value >> place) & 1)
    return 1.0 - 2.0 * (total & 1).astype(jnp.float32)


def hadamard(order):
    shape = (order, order)
    common = lax.broadcasted_iota(jnp.int32, shape, 0) & lax.broadcasted_iota(jnp.int32, shape, 1)
    return parity_sign(common, order.bit_length() - 1)


def butterfly(values):
    half = 1
    values = list(values)
    while half < len(values):
        for at in range(len(values)):
            if at & half == 0:
                low, high = values[at], values[at + half]
                values[at], values[at + half] = low + high, low - high
        half *= 2
    return values


def split_three(value):
    first = value.astype(jnp.bfloat16).astype(jnp.float32)
    rest = value - first
    second = rest.astype(jnp.bfloat16).astype(jnp.float32)
    return first, second, rest - second


def widen(value, width):
    return jnp.concatenate([value] * (width // COLS), axis=1)


def eliminate(rest, put):
    order, width = rest.shape
    row_at = lax.broadcasted_iota(jnp.int32, (BLOCK, COLS), 0)
    for step in range(order // BLOCK):
        base = step * BLOCK
        rows = rest[:BLOCK]
        columns = [
            jnp.broadcast_to(rows[:, base + m : base + m + 1], (BLOCK, COLS)) for m in range(BLOCK)
        ]
        pivots = jnp.ones((BLOCK, COLS), jnp.float32)
        for j in range(BLOCK):
            pivot = jnp.broadcast_to(columns[j][j : j + 1, :], (BLOCK, COLS))
            pivots = jnp.where(row_at == j, pivot, pivots)
            if j < BLOCK - 1:
                factor = jnp.where(row_at > j, columns[j] * (1.0 / pivot), 0.0)
                for m in range(j + 1, BLOCK):
                    columns[m] = columns[m] - factor * jnp.broadcast_to(
                        columns[m][j : j + 1, :], (BLOCK, COLS)
                    )
                rows = rows - widen(factor, width) * jnp.broadcast_to(
                    rows[j : j + 1, :], (BLOCK, width)
                )
        done = rows * widen(lax.rsqrt(pivots), width)
        put(base, done)
        if base + BLOCK < order:
            a, b, c = split_three(done)
            left = jnp.concatenate([t[:, :COLS] for t in (a, a, a, b, b, c)], axis=0)
            right = jnp.concatenate([a, b, c, a, b, a], axis=0).astype(jnp.bfloat16)
            turned = jnp.transpose(left)[base + BLOCK :, :].astype(jnp.bfloat16)
            rest = rest[BLOCK:] - jnp.dot(turned, right, preferred_element_type=jnp.float32)


def kernel(
    scale, samples, panel_hbm, sign_ref, index_hbm, q_ref, r_ref,
    panel, work, mix, index, away, near, home, land1, sum1, land2, sum2, land3, sketch,
    gram, gram_land, core_land, augmented,
    load_sem, index_sem, core_send, core_recv, s1, r1, s2, r2, s3, r3, gs, gr, gcs, gcr,
):
    hi, lo = lax.axis_index("hi"), lax.axis_index("lo")
    core = lo % 2
    place = (hi // 4, hi % 4, lo // 2)

    def device(coords, which):
        return (coords[0] * 4 + coords[1], coords[2] * 2 + which)

    def peer(axis, delta):
        coords = list(place)
        coords[axis] = coords[axis] ^ delta
        return device(coords, core)

    other = device(place, 1 - core)

    barrier = pltpu.get_barrier_semaphore()
    pl.semaphore_signal(barrier, inc=1, device_id=other, device_id_type=MESH)
    for axis in range(3):
        for delta in range(1, 4):
            pl.semaphore_signal(barrier, inc=1, device_id=peer(axis, delta), device_id_type=MESH)

    rows = panel.shape[0]
    outer = rows // MIX
    per_load = outer // LOADS
    piece = rows // LOADS

    def load(at):
        span = pl.ds(pl.multiple_of(at * piece, piece), piece)
        return pltpu.make_async_copy(panel_hbm.at[span], panel.at[span], load_sem.at[at])

    for at in range(LOADS):
        load(at).start()
    index_copy = pltpu.make_async_copy(index_hbm, index, index_sem)
    index_copy.start()
    mix[...] = hadamard(MIX).astype(jnp.bfloat16)

    def mix_group(at, carry):
        load(at).wait()
        for inner in range(per_load):
            start = pl.multiple_of((at * per_load + inner) * MIX, MIX)
            value = panel[pl.ds(start, MIX), :]
            high = value.astype(jnp.bfloat16)
            low = (value - high.astype(jnp.float32)).astype(jnp.bfloat16)
            signs = sign_ref[pl.ds(at * per_load + inner, 1), :].astype(jnp.float32)
            signed_mix = mix[...] * jnp.broadcast_to(signs, (MIX, MIX)).astype(jnp.bfloat16)
            mixed = jnp.dot(
                signed_mix, jnp.concatenate([high, low], axis=1), preferred_element_type=jnp.float32
            )
            work[pl.ds(start, MIX), :] = mixed[:, :COLS] + mixed[:, COLS:]
        return carry

    lax.fori_loop(0, LOADS, mix_group, 0)

    def butterflies(outer_stride, stride):
        def group(at, carry):
            def tile(t, carry):
                base = pl.multiple_of(at * outer_stride + t * 8, 8)
                spans = [pl.ds(pl.multiple_of(base + m * stride, 8), 8) for m in range(8)]
                for span, value in zip(spans, butterfly([work[span, :] for span in spans])):
                    work[span, :] = value
                return carry

            return lax.fori_loop(0, MIX // 8, tile, carry, unroll=4)

        lax.fori_loop(0, 8, group, 0)

    butterflies(8 * MIX, MIX)
    butterflies(MIX, 8 * MIX)
    index_copy.wait()

    def gather(target, part, delta, which):
        offset, count = PARTS[part]
        a, b, c = ORDERS[part]

        def one(j, carry):
            coords = [None] * 3
            coords[a] = place[a] ^ delta
            coords[b] = place[b] ^ (j // 4)
            coords[c] = place[c] ^ (j % 4)
            chip = coords[0] * 16 + coords[1] * 4 + coords[2]
            base = (chip * 2 + which) * samples + offset
            to = pl.multiple_of(j * count, 8)
            for k in range(count):
                row = index[base + k] & (rows - 1)
                target[part][pl.ds(delta * 16 * count + to + k, 1), :] = work[pl.ds(row, 1), :]
            return carry

        lax.fori_loop(0, 16, one, 0)

    def chunk(ref, part, delta):
        size = 16 * PARTS[part][1]
        return ref[part].at[pl.ds(delta * size, size)]

    def send(source, target, send_sem, recv_sem, to):
        return pltpu.make_async_remote_copy(
            src_ref=source, dst_ref=target, send_sem=send_sem, recv_sem=recv_sem,
            device_id=to, device_id_type=MESH,
        )

    pl.semaphore_wait(barrier, 10)
    sequence = [(part, delta) for delta in (1, 2, 3, 0) for part in range(3)]
    core_copies = {}
    for part, delta in sequence:
        gather(away, part, delta, 1 - core)
        at = part * 4 + delta
        copy = send(
            chunk(away, part, delta), chunk(near, part, delta),
            core_send.at[at], core_recv.at[at], other,
        )
        copy.start()
        core_copies[part, delta] = copy

    core_sign = 1.0 - 2.0 * core.astype(jnp.float32)
    copies1 = {}
    for part, delta in sequence:
        gather(home, part, delta, core)
        core_copies[part, delta].wait_recv()
        mine, theirs = chunk(home, part, delta), chunk(near, part, delta)
        mine[...] = theirs[...] + core_sign * mine[...]
        if delta:
            at = part * 3 + delta - 1
            size = 16 * PARTS[part][1]
            copy = send(
                mine, land1[part].at[pl.ds((delta - 1) * size, size)],
                s1.at[at], r1.at[at], peer(ORDERS[part][0], delta),
            )
            copy.start()
            copies1[part, delta] = copy

    def reduced(own, landed, size, axis, start, count):
        here = place[axis]
        total = parity_sign(here, 2) * own[pl.ds(start, count), :]
        for delta in range(1, 4):
            sign = parity_sign(here & (here ^ delta), 2)
            total = total + sign * landed[pl.ds((delta - 1) * size + start, count), :]
        return total

    copies2 = {}
    for part in range(3):
        count = PARTS[part][1]
        for delta in range(1, 4):
            copies1[part, delta].wait_recv()
        for delta in (1, 2, 3, 0):
            span = pl.ds(delta * 4 * count, 4 * count)
            sum1[part][span, :] = reduced(
                home[part], land1[part], 16 * count, ORDERS[part][0], delta * 4 * count, 4 * count
            )
            if delta:
                at = part * 3 + delta - 1
                copy = send(
                    sum1[part].at[span],
                    land2[part].at[pl.ds((delta - 1) * 4 * count, 4 * count)],
                    s2.at[at], r2.at[at], peer(ORDERS[part][1], delta),
                )
                copy.start()
                copies2[part, delta] = copy

    copies3 = {}
    for part in range(3):
        count = PARTS[part][1]
        for delta in range(1, 4):
            copies2[part, delta].wait_recv()
        for delta in (1, 2, 3, 0):
            span = pl.ds(delta * count, count)
            sum2[part][span, :] = reduced(
                sum1[part], land2[part], 4 * count, ORDERS[part][1], delta * count, count
            )
            if delta:
                at = part * 3 + delta - 1
                copy = send(
                    sum2[part].at[span], land3[part].at[pl.ds((delta - 1) * count, count)],
                    s3.at[at], r3.at[at], peer(ORDERS[part][2], delta),
                )
                copy.start()
                copies3[part, delta] = copy

    for part in range(3):
        offset, count = PARTS[part]
        for delta in range(1, 4):
            copies3[part, delta].wait_recv()
        sketch[pl.ds(offset, count), :] = scale * reduced(
            sum2[part], land3[part], count, ORDERS[part][2], 0, count
        )

    rows_here = jnp.concatenate(
        [sketch[...], jnp.zeros((COLS - samples, COLS), jnp.float32)], axis=0
    )
    turned = jnp.transpose(rows_here)
    device_total = lax.axis_size("hi") * lax.axis_size("lo")
    gram[0] = jnp.dot(
        turned, rows_here, precision=lax.Precision.HIGHEST, preferred_element_type=jnp.float32
    ) * (1.0 / (samples * device_total))

    core_gram = send(gram.at[0], core_land, gcs, gcr, other)
    core_gram.start()
    core_gram.wait_recv()
    gram[1] = gram[0] + core_land[...]
    gram_copies = []
    for stage in range(3):
        now = {}
        for part in range(3):
            offset, count = GRAM_PARTS[part]
            span = pl.ds(offset, count)
            for delta in range(1, 4):
                at = stage * 9 + part * 3 + delta - 1
                copy = send(
                    gram.at[stage + 1, span], gram_land.at[stage * 3 + delta - 1, span],
                    gs.at[at], gr.at[at], peer(ORDERS[part][stage], delta),
                )
                copy.start()
                now[part, delta] = copy
                gram_copies.append(copy)
        for part in range(3):
            offset, count = GRAM_PARTS[part]
            span = pl.ds(offset, count)
            for delta in range(1, 4):
                now[part, delta].wait_recv()
            own = gram[stage + 1, span, :]
            one, two, three = (gram_land[stage * 3 + d, span, :] for d in range(3))
            gram[stage + 2, span, :] = (own + two) + (one + three)

    def put(base, value):
        augmented[base : base + BLOCK, :] = value

    eliminate(jnp.concatenate([gram[4], turned], axis=1), put)
    row_at = lax.broadcasted_iota(jnp.int32, (COLS, COLS), 0)
    col_at = lax.broadcasted_iota(jnp.int32, (COLS, COLS), 1)
    r_ref[...] = jnp.where(row_at <= col_at, augmented[:, :COLS], 0.0)
    q_ref[...] = jnp.transpose(augmented[:, COLS:])[:samples, :]

    for group in (core_copies, copies1, copies2, copies3):
        for copy in group.values():
            copy.wait_send()
    core_gram.wait_send()
    for copy in gram_copies:
        copy.wait_send()


def shards(panel, signs, sample_rows):
    rows, cols = panel.shape
    devices = lax.axis_size(("hi", "lo"))
    samples = sample_rows.shape[0] // devices
    counts = [count for _, count in PARTS]
    f32 = jnp.float32

    def buffers(blocks):
        return [pltpu.VMEM((blocks * count, cols), f32) for count in counts]

    dma = pltpu.SemaphoreType.DMA
    vmem = pl.BlockSpec(memory_space=pltpu.VMEM)
    hbm = pl.BlockSpec(memory_space=pl.ANY)
    return pl.pallas_call(
        functools.partial(kernel, 1.0 / math.sqrt(rows * devices), samples),
        out_shape=(
            jax.ShapeDtypeStruct((samples, cols), f32),
            jax.ShapeDtypeStruct((cols, cols), f32),
        ),
        in_specs=[hbm, vmem, hbm],
        out_specs=(vmem, vmem),
        scratch_shapes=[
            pltpu.VMEM((rows, cols), f32),
            pltpu.VMEM((rows, cols), f32),
            pltpu.VMEM((MIX, MIX), jnp.bfloat16),
            pltpu.SMEM(sample_rows.shape, jnp.int32),
            buffers(64), buffers(64), buffers(64),
            buffers(48), buffers(16), buffers(12), buffers(4), buffers(3),
            pltpu.VMEM((samples, cols), f32),
            pltpu.VMEM((5, cols, cols), f32),
            pltpu.VMEM((9, cols, cols), f32),
            pltpu.VMEM((cols, cols), f32),
            pltpu.VMEM((cols, 2 * cols), f32),
            dma((LOADS,)), dma, dma((12,)), dma((12,)),
            dma((9,)), dma((9,)), dma((9,)), dma((9,)), dma((9,)), dma((9,)),
            dma((27,)), dma((27,)), dma, dma,
        ],
        compiler_params=pltpu.CompilerParams(
            collective_id=0, has_side_effects=True, vmem_limit_bytes=48 * 2**20
        ),
        name="sketch_qr",
    )(panel, signs.reshape(rows // MIX, MIX), sample_rows)


def solution(mesh):
    placed = (P(("hi", "lo"), None), P(("hi", "lo")), P())
    return jax.shard_map(
        shards, mesh=mesh, in_specs=placed, out_specs=(P(("hi", "lo"), None), P()), check_vma=False
    )
```

time: 689 us -> 64.9 us (0.09); the launches traced: 676 us -> 64.7 us
  blocking collectives: 302 us -> 0 us
  waiting for transfers between devices: 254 us -> 0 us
  Pallas kernels: 0 us -> 61.1 us
  matrix products: 53.8 us -> 0 us
  other arithmetic: 34.9 us -> 0 us
  between operations: 14.3 us -> 0.65 us
  local copies, waits for them, and re-layouts: 12.4 us -> 2.86 us
    all_to_all x3 -> x0, blocking collectives: 302 us -> none  [the longest x1 103 us: shards(): lax.all_to_all(shuffled, 'hi', split_axis=1, concat_axis=0, tiled=True)]
    psum x1 -> x0, waiting for transfers between devices: 133 us -> none  [shards(): gram = lax.psum(partial_gram, ('hi', 'lo')) / (per_device * device_count)]
    all_to_all x1 -> x0, waiting for transfers between devices: 121 us -> none  [shards(): lax.all_to_all(shuffled, 'hi', split_axis=0, concat_axis=1, tiled=True)]
    pallas_call x0 -> x1, Pallas kernels: none -> 61.1 us  [shards(): pl.pallas_call(functools.partial(kernel, 1.0 / math.sqrt(rows * devices),...]
    dot_general x5 -> x0, matrix products: 53 us -> none  [the longest x1 14 us: shards(): jnp.einsum('ij,jrc->irc', hadamard(width_lo), shuffled, precision=highest)]
    another operation x4 -> x0, other arithmetic: 22.2 us -> none  [the longest x3 12.4 us: shards(): lower = jnp.linalg.cholesky(gram)]
    mul x1 -> x0, other arithmetic: 8.68 us -> none  [shards(): signed = panel * signs[:, None].astype(jnp.float32)]
    dot_general x2 -> x0, local copies, waits for them, and re-layouts: 7.56 us -> none  [the longest x1 5.94 us: shards(): jnp.einsum('ij,jrc->irc', hadamard(width_hi), shuffled, precision=highest)]
  transfers between devices with their start and end apart: 2 -> 0, of which waited for: 2 -> 0; matrix products, arithmetic and copies ran while one was open for 0% -> 0% of each run, Pallas kernels for 0% -> 0%
where the time goes in v1:
time: 64.9 us; the launch traced here: 64.7 us
  Pallas kernels  61.1 us (94%)
  local copies, waits for them, and re-layouts  2.86 us (4%)
  between operations  0.65 us (1%)
    pallas_call x1, Pallas kernels, shards(): pl.pallas_call(functools.partial(kernel, 1.0 / math.sqrt(rows * devices),...  61.1 us
    unnamed x4, local copies, waits for them, and re-layouts  2 us

profile of v1, /device:TPU:0, one launch (start us, length us, event | category | flops | bytes accessed | tf_op | source)
XLA Modules:
  0.0 64.7 jit_solution(7235394719043975496)
XLA Ops:
  0.6 0.9 %reshape.7.sign_ref = s32[64,256]{1,0:T(8,128)S(1)} reshape(s32[16384]{0:T(1024)} %param.4) | data formatting | bytes 131072 | tf_op jit(solution)/shard_map/reshape | solution.py:373
  1.5 0.0 copy-start
  1.5 0.7 %copy-done = s32[8192]{0:T(1024)S(1)} copy-done((s32[8192]{0:T(1024)S(1)}, s32[8192]{0:T(1024)}, u32[]{:S(2)}) %copy-start) | copy-done | bytes 32792
  2.3 61.1 %sketch_qr.1 = (f32[64,128]{1,0:T(8,128)S(1)}, f32[128,128]{1,0:T(8,128)S(1)}) custom-call(f32[16384,128]{1,0:T(8,128)} %panel_hbm.1, s32[64,256]{1,0:T(8,128)S(1)} %reshape.7.sign_ref, s32[8192]{0:T(1024)S(1)} %copy-done), custom_call_target="tpu_custom_call" | custom-call | tf_op jit(solution)/shard_map/sketch_qr/pallas_call | solution.py:345
  63.4 0.6 copy.7
  64.0 0.6 copy.8
Async XLA Ops:
  1.5 0.8 %copy-start = (s32[8192]{0:T(1024)S(1)}, s32[8192]{0:T(1024)}, u32[]{:S(2)}) copy-start(s32[8192]{0:T(1024)} %index_hbm.1) | copy-start | bytes 98308

commit v2 on v1

--- a/solution.py
+++ b/solution.py
@@ -87,10 +87,10 @@
 
 
 def kernel(
-    scale, samples, panel_hbm, sign_ref, index_hbm, q_ref, r_ref,
-    panel, work, mix, index, away, near, home, land1, sum1, land2, sum2, land3, sketch,
+    scale, samples, panel_hbm, sign_hbm, index_hbm, q_ref, r_ref,
+    panel, work, mix, sign_ref, index, away, near, home, land1, sum1, land2, sum2, land3, sketch,
     gram, gram_land, core_land, augmented,
-    load_sem, index_sem, core_send, core_recv, s1, r1, s2, r2, s3, r3, gs, gr, gcs, gcr,
+    load_sem, sign_sem, index_sem, core_send, core_recv, s1, r1, s2, r2, s3, r3, gs, gr, gcs, gcr,
 ):
     hi, lo = lax.axis_index("hi"), lax.axis_index("lo")
     core = lo % 2
@@ -121,11 +121,14 @@
         span = pl.ds(pl.multiple_of(at * piece, piece), piece)
         return pltpu.make_async_copy(panel_hbm.at[span], panel.at[span], load_sem.at[at])
 
+    sign_copy = pltpu.make_async_copy(sign_hbm, sign_ref, sign_sem)
+    sign_copy.start()
     for at in range(LOADS):
         load(at).start()
     index_copy = pltpu.make_async_copy(index_hbm, index, index_sem)
     index_copy.start()
     mix[...] = hadamard(MIX).astype(jnp.bfloat16)
+    sign_copy.wait()
 
     def mix_group(at, carry):
         load(at).wait()
@@ -134,7 +137,10 @@
             value = panel[pl.ds(start, MIX), :]
             high = value.astype(jnp.bfloat16)
             low = (value - high.astype(jnp.float32)).astype(jnp.bfloat16)
-            signs = sign_ref[pl.ds(at * per_load + inner, 1), :].astype(jnp.float32)
+            line = (at * per_load + inner) * (MIX // COLS)
+            signs = jnp.concatenate(
+                [sign_ref[pl.ds(line + m, 1), :] for m in range(MIX // COLS)], axis=1
+            ).astype(jnp.float32)
             signed_mix = mix[...] * jnp.broadcast_to(signs, (MIX, MIX)).astype(jnp.bfloat16)
             mixed = jnp.dot(
                 signed_mix, jnp.concatenate([high, low], axis=1), preferred_element_type=jnp.float32
@@ -192,8 +198,10 @@
 
     pl.semaphore_wait(barrier, 10)
     sequence = [(part, delta) for delta in (1, 2, 3, 0) for part in range(3)]
-    core_copies = {}
-    for part, delta in sequence:
+    core_sign = 1.0 - 2.0 * core.astype(jnp.float32)
+    core_copies, copies1 = {}, {}
+
+    def give(part, delta):
         gather(away, part, delta, 1 - core)
         at = part * 4 + delta
         copy = send(
@@ -203,9 +211,7 @@
         copy.start()
         core_copies[part, delta] = copy
 
-    core_sign = 1.0 - 2.0 * core.astype(jnp.float32)
-    copies1 = {}
-    for part, delta in sequence:
+    def keep(part, delta):
         gather(home, part, delta, core)
         core_copies[part, delta].wait_recv()
         mine, theirs = chunk(home, part, delta), chunk(near, part, delta)
@@ -219,6 +225,12 @@
             )
             copy.start()
             copies1[part, delta] = copy
+
+    give(*sequence[0])
+    for at, step in enumerate(sequence):
+        if at + 1 < len(sequence):
+            give(*sequence[at + 1])
+        keep(*step)
 
     def reduced(own, landed, size, axis, start, count):
         here = place[axis]
@@ -341,19 +353,20 @@
 
     dma = pltpu.SemaphoreType.DMA
     vmem = pl.BlockSpec(memory_space=pltpu.VMEM)
-    hbm = pl.BlockSpec(memory_space=pl.ANY)
+    hbm = pl.BlockSpec(memory_space=pltpu.HBM)
     return pl.pallas_call(
         functools.partial(kernel, 1.0 / math.sqrt(rows * devices), samples),
         out_shape=(
             jax.ShapeDtypeStruct((samples, cols), f32),
             jax.ShapeDtypeStruct((cols, cols), f32),
         ),
-        in_specs=[hbm, vmem, hbm],
+        in_specs=[hbm, hbm, hbm],
         out_specs=(vmem, vmem),
         scratch_shapes=[
             pltpu.VMEM((rows, cols), f32),
             pltpu.VMEM((rows, cols), f32),
             pltpu.VMEM((MIX, MIX), jnp.bfloat16),
+            pltpu.VMEM((rows // COLS, COLS), jnp.int32),
             pltpu.SMEM(sample_rows.shape, jnp.int32),
             buffers(64), buffers(64), buffers(64),
             buffers(48), buffers(16), buffers(12), buffers(4), buffers(3),
@@ -362,15 +375,15 @@
             pltpu.VMEM((9, cols, cols), f32),
             pltpu.VMEM((cols, cols), f32),
             pltpu.VMEM((cols, 2 * cols), f32),
-            dma((LOADS,)), dma, dma((12,)), dma((12,)),
+            dma((LOADS,)), dma, dma, dma((12,)), dma((12,)),
             dma((9,)), dma((9,)), dma((9,)), dma((9,)), dma((9,)), dma((9,)),
             dma((27,)), dma((27,)), dma, dma,
         ],
         compiler_params=pltpu.CompilerParams(
-            collective_id=0, has_side_effects=True, vmem_limit_bytes=48 * 2**20
+            collective_id=0, has_side_effects=True, vmem_limit_bytes=63 * 2**20
         ),
         name="sketch_qr",
-    )(panel, signs.reshape(rows // MIX, MIX), sample_rows)
+    )(panel, signs.reshape(rows // COLS, COLS), sample_rows)
 
 
 def solution(mesh):

time: 64.9 us -> 62.7 us (0.966)
  Pallas kernels: 61.1 us -> 59 us
    pallas_call x1, Pallas kernels: 61.1 us -> 59 us  [shards(): pl.pallas_call(functools.partial(kernel, 1.0 / math.sqrt(rows * devices),...]
    reshape x1 -> x0, local copies, waits for them, and re-layouts: 0.86 us -> none  [shards(): signs.reshape(rows // MIX, MIX)]
    unnamed x4 -> x2, local copies, waits for them, and re-layouts: 2 us -> 2.85 us
where the time goes in v2:
time: 62.7 us; the launch traced here: 62.5 us
  Pallas kernels  59 us (94%)
  local copies, waits for them, and re-layouts  2.85 us (5%)
  between operations  0.64 us (1%)
    pallas_call x1, Pallas kernels, shards(): pl.pallas_call(functools.partial(kernel, 1.0 / math.sqrt(rows * devices),...  59 us
    unnamed x2, local copies, waits for them, and re-layouts  2.85 us

profile of v2, /device:TPU:0, one launch (start us, length us, event | category | flops | bytes accessed | tf_op | source)
XLA Modules:
  0.0 62.5 jit_solution(1867087410216966307)
XLA Ops:
  0.6 59.0 %sketch_qr.1 = (f32[64,128]{1,0:T(8,128)}, f32[128,128]{1,0:T(8,128)}) custom-call(f32[16384,128]{1,0:T(8,128)} %panel_hbm.1, s32[128,128]{1,0:T(8,128)} %bitcast.1, s32[8192]{0:T(1024)} %index_hbm.1), custom_call_target="tpu_custom_call" | custom-call | tf_op jit(solution)/shard_map/sketch_qr/pallas_call | solution.py:357
  59.7 1.4 %copy.7 = f32[64,128]{1,0:T(8,128)} copy(f32[64,128]{1,0:T(8,128)} %get-tuple-element.4) | data formatting | bytes 65536
  61.0 1.5 %copy.8 = f32[128,128]{1,0:T(8,128)} copy(f32[128,128]{1,0:T(8,128)} %get-tuple-element.5) | data formatting | bytes 131072

commit v3 on v2

v3 whole, which is shorter than its diff:
```python
import functools
import math

import jax
import jax.numpy as jnp
from jax import lax
from jax.experimental import pallas as pl
from jax.experimental.pallas import tpu as pltpu
from jax.sharding import PartitionSpec as P

MESH = pl.DeviceIdType.MESH
COLS = 128
MIX = 128
LOADS = 8
BLOCK = 16
PART = 24
GRAM_PART = 48
DELTAS = 0x36
AHEAD = 3


def parity_sign(value, bits):
    total = value & 1
    for place in range(1, bits):
        total = total + ((value >> place) & 1)
    return 1.0 - 2.0 * (total & 1).astype(jnp.float32)


def hadamard(order):
    shape = (order, order)
    common = lax.broadcasted_iota(jnp.int32, shape, 0) & lax.broadcasted_iota(jnp.int32, shape, 1)
    return parity_sign(common, order.bit_length() - 1)


def butterfly(values):
    half = 1
    values = list(values)
    while half < len(values):
        for at in range(len(values)):
            if at & half == 0:
                low, high = values[at], values[at + half]
                values[at], values[at + half] = low + high, low - high
        half *= 2
    return values


def split_three(value):
    first = value.astype(jnp.bfloat16).astype(jnp.float32)
    rest = value - first
    second = rest.astype(jnp.bfloat16).astype(jnp.float32)
    return first, second, rest - second


def widen(value, width):
    return jnp.concatenate([value] * (width // COLS), axis=1)


def eliminate(rest, put):
    order, width = rest.shape
    row_at = lax.broadcasted_iota(jnp.int32, (BLOCK, COLS), 0)
    for step in range(order // BLOCK):
        base = step * BLOCK
        rows = rest[:BLOCK]
        columns = [
            jnp.broadcast_to(rows[:, base + m : base + m + 1], (BLOCK, COLS)) for m in range(BLOCK)
        ]
        pivots = jnp.ones((BLOCK, COLS), jnp.float32)
        for j in range(BLOCK):
            pivot = jnp.broadcast_to(columns[j][j : j + 1, :], (BLOCK, COLS))
            pivots = jnp.where(row_at == j, pivot, pivots)
            if j < BLOCK - 1:
                factor = jnp.where(row_at > j, columns[j] * (1.0 / pivot), 0.0)
                for m in range(j + 1, BLOCK):
                    columns[m] = columns[m] - factor * jnp.broadcast_to(
                        columns[m][j : j + 1, :], (BLOCK, COLS)
                    )
                rows = rows - widen(factor, width) * jnp.broadcast_to(
                    rows[j : j + 1, :], (BLOCK, width)
                )
        done = rows * widen(lax.rsqrt(pivots), width)
        put(base, done)
        if base + BLOCK < order:
            a, b, c = split_three(done)
            left = jnp.concatenate([t[:, :COLS] for t in (a, a, a, b, b, c)], axis=0)
            right = jnp.concatenate([a, b, c, a, b, a], axis=0).astype(jnp.bfloat16)
            turned = jnp.transpose(left)[base + BLOCK :, :].astype(jnp.bfloat16)
            rest = rest[BLOCK:] - jnp.dot(turned, right, preferred_element_type=jnp.float32)


def kernel(
    scale, samples, panel_hbm, sign_hbm, index_hbm, q_ref, r_ref,
    panel, work, mix, sign_ref, index_rows, index, away, near, home, land1, sum1, land2, sum2, land3, sketch,
    gram, gram_land, core_land, augmented,
    load_sem, sign_sem, index_sem, core_send, core_recv, s1, r1, s2, r2, s3, r3, gs, gr, gcs, gcr,
):
    core = lax.axis_index("lo") % 2
    chip = lax.axis_index("hi") * 4 + lax.axis_index("lo") // 2
    rows = panel.shape[0]

    def device(which_chip, which_core):
        return (which_chip // 4, (which_chip % 4) * 2 + which_core)

    def shift(part, level):
        return 4 - 2 * ((part + level) % 3)

    def peer(part, level, delta):
        return device(chip ^ (delta << shift(part, level)), core)

    def sign(part, level, delta):
        here = (chip >> shift(part, level)) & 3
        return parity_sign(here & (here ^ delta), 2)

    def split_step(step):
        return step % 3, (DELTAS >> (2 * (step // 3))) & 3

    def block(ref, at, count):
        return ref.at[pl.ds(pl.multiple_of(at * count, 8), count)]

    other = device(chip, 1 - core)
    barrier = pltpu.get_barrier_semaphore()
    pl.semaphore_signal(barrier, inc=1, device_id=other, device_id_type=MESH)

    def greet(step, carry):
        pl.semaphore_signal(
            barrier, inc=1, device_id=peer(step % 3, 0, step // 3 + 1), device_id_type=MESH
        )
        return carry

    lax.fori_loop(0, 9, greet, 0)

    outer = rows // MIX
    per_load = outer // LOADS
    piece = rows // LOADS

    def load(at):
        span = pl.ds(pl.multiple_of(at * piece, piece), piece)
        return pltpu.make_async_copy(panel_hbm.at[span], panel.at[span], load_sem.at[at])

    sign_copy = pltpu.make_async_copy(sign_hbm, sign_ref, sign_sem)
    sign_copy.start()
    for at in range(LOADS):
        load(at).start()
    index_copy = pltpu.make_async_copy(index_hbm, index_rows, index_sem)
    index_copy.start()
    mix[...] = hadamard(MIX).astype(jnp.bfloat16)
    sign_copy.wait()

    def mix_group(at, carry):
        load(at).wait()
        for inner in range(per_load):
            line = at * per_load + inner
            start = pl.multiple_of(line * MIX, MIX)
            value = panel[pl.ds(start, MIX), :]
            high = value.astype(jnp.bfloat16)
            low = (value - high.astype(jnp.float32)).astype(jnp.bfloat16)
            signs = sign_ref[pl.ds(line, 1), :].astype(jnp.float32)
            signed_mix = mix[...] * jnp.broadcast_to(signs, (MIX, MIX)).astype(jnp.bfloat16)
            work[pl.ds(start, MIX), :] = jnp.dot(
                jnp.concatenate([signed_mix, signed_mix], axis=1),
                jnp.concatenate([high, low], axis=0),
                preferred_element_type=jnp.float32,
            )
        return carry

    lax.fori_loop(0, LOADS, mix_group, 0)
    index_copy.wait()
    index_rows[...] = index_rows[...] & (rows - 1)
    index_move = pltpu.make_async_copy(index_rows, index, index_sem)
    index_move.start()

    def butterflies(order, outer_stride, stride, unroll):
        def group(at, carry):
            def tile(t, carry):
                base = pl.multiple_of(at * outer_stride + t * 8, 8)
                spans = [pl.ds(pl.multiple_of(base + m * stride, 8), 8) for m in range(order)]
                for span, value in zip(spans, butterfly([work[span, :] for span in spans])):
                    work[span, :] = value
                return carry

            return lax.fori_loop(0, MIX // 8, tile, carry, unroll=unroll)

        lax.fori_loop(0, outer // order, group, 0)

    butterflies(per_load, per_load * MIX, MIX, 2)
    butterflies(LOADS, MIX, per_load * MIX, 4)
    index_move.wait()

    def gather(step, which, write):
        part, delta = split_step(step)
        count = min(PART, samples - part * PART)

        def one(j, carry):
            for inner in range(4):
                to_chip = chip ^ (
                    (delta << shift(part, 0)) | (j << shift(part, 1)) | (inner << shift(part, 2))
                )
                base = (to_chip * 2 + which) * samples + part * PART
                to = pl.multiple_of(step * 16 * PART + (j * 4 + inner) * PART, 8)
                for k in range(count):
                    write(to + k, work[pl.ds(index[base + k], 1), :])
            return carry

        lax.fori_loop(0, 4, one, 0)

    def send(source, target, send_sem, recv_sem, to):
        return pltpu.make_async_remote_copy(
            src_ref=source, dst_ref=target, send_sem=send_sem, recv_sem=recv_sem,
            device_id=to, device_id_type=MESH,
        )

    def core_copy(step):
        return send(
            block(away, step, 16 * PART), block(near, step, 16 * PART),
            core_send.at[step], core_recv.at[step], other,
        )

    def part_copy(source, target, count, sends, recvs, level, step):
        part, delta = split_step(step)
        return send(
            block(source, step, count), block(target, step, count),
            sends.at[step], recvs.at[step], peer(part, level, delta),
        )

    copy1 = functools.partial(part_copy, home, land1, 16 * PART, s1, r1, 0)
    copy2 = functools.partial(part_copy, sum1, land2, 4 * PART, s2, r2, 1)
    copy3 = functools.partial(part_copy, sum2, land3, PART, s3, r3, 2)
    core_sign = 1.0 - 2.0 * core.astype(jnp.float32)

    def write_away(to, value):
        away[pl.ds(to, 1), :] = value

    def write_home(to, value):
        home[pl.ds(to, 1), :] = near[pl.ds(to, 1), :] + core_sign * value

    pl.semaphore_wait(barrier, 10)

    for at in range(12 + AHEAD):
        if at < 12:
            gather(at, 1 - core, write_away)
            core_copy(at).start()
        if at >= AHEAD:
            step = at - AHEAD
            core_copy(step).wait_recv()
            gather(step, core, write_home)
            if step < 9:
                copy1(step).start()

    def total(own, landed, part, level, own_at, land_at, land_stride):
        out = sign(part, level, 0) * own[pl.ds(own_at, 8), :]
        for hop in range(3):
            delta = (DELTAS >> (2 * hop)) & 3
            at = pl.multiple_of(land_at + hop * land_stride, 8)
            out = out + sign(part, level, delta) * landed[pl.ds(at, 8), :]
        return out

    def fold(own, landed, count, level, copy_in, target, copy_out):
        whole = 4 * count

        def one(step, carry):
            part, delta = split_step(step)

            @pl.when(step < 3)
            def _():
                for hop in range(3):
                    copy_in(hop * 3 + part).wait_recv()

            def tile(t, carry):
                inside = delta * count + t * 8
                target[pl.ds(pl.multiple_of(step * count + t * 8, 8), 8), :] = total(
                    own, landed, part, level,
                    pl.multiple_of((9 + part) * whole + inside, 8), part * whole + inside, 3 * whole,
                )
                return carry

            lax.fori_loop(0, count // 8, tile, 0, unroll=3)

            @pl.when(step < 9)
            def _():
                copy_out(step).start()

            return carry

        lax.fori_loop(0, 12, one, 0)

    fold(home, land1, 4 * PART, 0, copy1, sum1, copy2)
    fold(sum1, land2, PART, 1, copy2, sum2, copy3)

    def finish(part, carry):
        for hop in range(3):
            copy3(hop * 3 + part).wait_recv()
        for t in range(PART // 8):
            inside = part * PART + t * 8
            sketch[pl.ds(pl.multiple_of(inside, 8), 8), :] = scale * total(
                sum2, land3, part, 2, pl.multiple_of(9 * PART + inside, 8), inside, 3 * PART
            )
        return carry

    lax.fori_loop(0, 3, finish, 0)

    rows_here = jnp.concatenate(
        [sketch[:samples, :], jnp.zeros((COLS - samples, COLS), jnp.float32)], axis=0
    )
    turned = jnp.transpose(rows_here)
    device_total = lax.axis_size("hi") * lax.axis_size("lo")
    gram[0, :COLS, :] = jnp.dot(
        turned, rows_here, precision=lax.Precision.HIGHEST, preferred_element_type=jnp.float32
    ) * (1.0 / (samples * device_total))
    gram[0, COLS:, :] = jnp.zeros((3 * GRAM_PART - COLS, COLS), jnp.float32)

    core_gram = send(gram.at[0], core_land, gcs, gcr, other)
    core_gram.start()
    core_gram.wait_recv()
    gram[1] = gram[0] + core_land[...]

    def gram_copy(stage, step):
        part, delta = split_step(step)
        span = pl.ds(pl.multiple_of(part * GRAM_PART, 8), GRAM_PART)
        at = stage * 9 + step
        return send(
            gram.at[stage + 1, span], gram_land.at[stage * 3 + step // 3, span],
            gs.at[at], gr.at[at], peer(part, stage, delta),
        )

    def gram_stage(stage, carry):
        def start(step, carry):
            gram_copy(stage, step).start()
            return carry

        lax.fori_loop(0, 9, start, 0)

        def add(part, carry):
            for hop in range(3):
                gram_copy(stage, hop * 3 + part).wait_recv()
            for t in range(GRAM_PART // 8):
                span = pl.ds(pl.multiple_of(part * GRAM_PART + t * 8, 8), 8)
                own = gram[stage + 1, span, :]
                two, one, three = (gram_land[stage * 3 + hop, span, :] for hop in range(3))
                gram[stage + 2, span, :] = (own + two) + (one + three)
            return carry

        return lax.fori_loop(0, 3, add, carry)

    lax.fori_loop(0, 3, gram_stage, 0)

    def put(base, value):
        augmented[base : base + BLOCK, :] = value

    eliminate(jnp.concatenate([gram[4, :COLS, :], turned], axis=1), put)
    row_at = lax.broadcasted_iota(jnp.int32, (COLS, COLS), 0)
    col_at = lax.broadcasted_iota(jnp.int32, (COLS, COLS), 1)
    r_ref[...] = jnp.where(row_at <= col_at, augmented[:, :COLS], 0.0)
    q_ref[...] = jnp.transpose(augmented[:, COLS:])[:samples, :]

    def drain_core(step, carry):
        core_copy(step).wait_send()
        return carry

    def drain(step, carry):
        for copy in (copy1, copy2, copy3):
            copy(step).wait_send()
        for stage in range(3):
            gram_copy(stage, step).wait_send()
        return carry

    lax.fori_loop(0, 12, drain_core, 0)
    lax.fori_loop(0, 9, drain, 0)
    core_gram.wait_send()


def shards(panel, signs, sample_rows):
    rows, cols = panel.shape
    devices = lax.axis_size(("hi", "lo"))
    samples = sample_rows.shape[0] // devices
    f32 = jnp.float32

    def buffers(blocks):
        return pltpu.VMEM((blocks * 3 * PART, cols), f32)

    dma = pltpu.SemaphoreType.DMA
    vmem = pl.BlockSpec(memory_space=pltpu.VMEM)
    hbm = pl.BlockSpec(memory_space=pltpu.HBM)
    return pl.pallas_call(
        functools.partial(kernel, 1.0 / math.sqrt(rows * devices), samples),
        out_shape=(
            pltpu.VMEM((samples, cols), f32),
            pltpu.VMEM((cols, cols), f32),
        ),
        in_specs=[hbm, hbm, hbm],
        out_specs=(vmem, vmem),
        scratch_shapes=[
            pltpu.VMEM((rows, cols), f32),
            pltpu.VMEM((rows, cols), f32),
            pltpu.VMEM((MIX, MIX), jnp.bfloat16),
            pltpu.VMEM((rows // COLS, COLS), jnp.int32),
            pltpu.VMEM(sample_rows.shape, jnp.int32),
            pltpu.SMEM(sample_rows.shape, jnp.int32),
            buffers(64), buffers(64), buffers(64),
            buffers(48), buffers(16), buffers(12), buffers(4), buffers(3),
            pltpu.VMEM((3 * PART, cols), f32),
            pltpu.VMEM((5, 3 * GRAM_PART, cols), f32),
            pltpu.VMEM((9, 3 * GRAM_PART, cols), f32),
            pltpu.VMEM((3 * GRAM_PART, cols), f32),
            pltpu.VMEM((cols, 2 * cols), f32),
            dma((LOADS,)), dma, dma, dma((12,)), dma((12,)),
            dma((9,)), dma((9,)), dma((9,)), dma((9,)), dma((9,)), dma((9,)),
            dma((27,)), dma((27,)), dma, dma,
        ],
        compiler_params=pltpu.CompilerParams(
            collective_id=0, has_side_effects=True, vmem_limit_bytes=63 * 2**20
        ),
        name="sketch_qr",
    )(panel, signs.reshape(rows // COLS, COLS), sample_rows)


def solution(mesh):
    placed = (P(("hi", "lo"), None), P(("hi", "lo")), P())
    return jax.shard_map(
        shards, mesh=mesh, in_specs=placed, out_specs=(P(("hi", "lo"), None), P()), check_vma=False
    )
```

time: 62.7 us -> 57.5 us (0.917)
  Pallas kernels: 59 us -> 55.2 us
  local copies, waits for them, and re-layouts: 2.85 us -> 1.25 us
    pallas_call x1, Pallas kernels: 59 us -> 55.2 us  [shards(): pl.pallas_call(functools.partial(kernel, 1.0 / math.sqrt(rows * devices),...]
    unnamed x2, local copies, waits for them, and re-layouts: 2.85 us -> 1.25 us
where the time goes in v3:
time: 57.5 us; the launch traced here: 57.1 us
  Pallas kernels  55.2 us (96%)
  local copies, waits for them, and re-layouts  1.25 us (2%)
  between operations  0.64 us (1%)
    pallas_call x1, Pallas kernels, shards(): pl.pallas_call(functools.partial(kernel, 1.0 / math.sqrt(rows * devices),...  55.2 us
    unnamed x2, local copies, waits for them, and re-layouts  1.25 us

profile of v3, /device:TPU:0, one launch (start us, length us, event | category | flops | bytes accessed | tf_op | source)
XLA Modules:
  0.0 57.1 jit_solution(16300374954978197832)
XLA Ops:
  0.6 55.2 %sketch_qr.1 = (f32[64,128]{1,0:T(8,128)S(1)}, f32[128,128]{1,0:T(8,128)S(1)}) custom-call(f32[16384,128]{1,0:T(8,128)} %panel_hbm.1, s32[128,128]{1,0:T(8,128)} %bitcast.1, s32[8192]{0:T(1024)} %index_hbm.1), custom_call_target="tpu_custom_call" | custom-call | tf_op jit(solution)/shard_map/sketch_qr/pallas_call | solution.py:382
  55.9 0.6 %copy.7 = f32[64,128]{1,0:T(8,128)} copy(f32[64,128]{1,0:T(8,128)S(1)} %get-tuple-element.2) | data formatting | bytes 65536
  56.5 0.6 %copy.8 = f32[128,128]{1,0:T(8,128)} copy(f32[128,128]{1,0:T(8,128)S(1)} %get-tuple-element.3) | data formatting | bytes 131072

commit v4 on v3

--- a/solution.py
+++ b/solution.py
@@ -14,7 +14,9 @@
 LOADS = 8
 BLOCK = 16
 PART = 24
-GRAM_PART = 48
+GRAM_PART = 32
+IN_FLIGHT = 4
+PIECES = 2
 DELTAS = 0x36
 AHEAD = 3
 
@@ -101,7 +103,8 @@
         return (which_chip // 4, (which_chip % 4) * 2 + which_core)
 
     def shift(part, level):
-        return 4 - 2 * ((part + level) % 3)
+        axis = part + level
+        return 4 - 2 * (axis % 3) if isinstance(axis, int) else 4 - 2 * lax.rem(axis, 3)
 
     def peer(part, level, delta):
         return device(chip ^ (delta << shift(part, level)), core)
@@ -114,7 +117,7 @@
         return step % 3, (DELTAS >> (2 * (step // 3))) & 3
 
     def block(ref, at, count):
-        return ref.at[pl.ds(pl.multiple_of(at * count, 8), count)]
+        return ref.at[pl.ds(at * count if isinstance(at, int) else pl.multiple_of(at * count, 8), count)]
 
     other = device(chip, 1 - core)
     barrier = pltpu.get_barrier_semaphore()
@@ -138,7 +141,7 @@
 
     sign_copy = pltpu.make_async_copy(sign_hbm, sign_ref, sign_sem)
     sign_copy.start()
-    for at in range(LOADS):
+    for at in range(IN_FLIGHT):
         load(at).start()
     index_copy = pltpu.make_async_copy(index_hbm, index_rows, index_sem)
     index_copy.start()
@@ -147,6 +150,11 @@
 
     def mix_group(at, carry):
         load(at).wait()
+
+        @pl.when(at + IN_FLIGHT < LOADS)
+        def _():
+            load(at + IN_FLIGHT).start()
+
         for inner in range(per_load):
             line = at * per_load + inner
             start = pl.multiple_of(line * MIX, MIX)
@@ -185,7 +193,7 @@
     butterflies(LOADS, MIX, per_load * MIX, 4)
     index_move.wait()
 
-    def gather(step, which, write):
+    def gather(step, cut, which, write):
         part, delta = split_step(step)
         count = min(PART, samples - part * PART)
 
@@ -200,7 +208,7 @@
                     write(to + k, work[pl.ds(index[base + k], 1), :])
             return carry
 
-        lax.fori_loop(0, 4, one, 0)
+        lax.fori_loop(cut * 4 // PIECES, (cut + 1) * 4 // PIECES, one, 0)
 
     def send(source, target, send_sem, recv_sem, to):
         return pltpu.make_async_remote_copy(
@@ -208,10 +216,19 @@
             device_id=to, device_id_type=MESH,
         )
 
-    def core_copy(step):
+    def core_copy(step, cut):
+        at, size = step * PIECES + cut, 16 * PART // PIECES
         return send(
-            block(away, step, 16 * PART), block(near, step, 16 * PART),
-            core_send.at[step], core_recv.at[step], other,
+            block(away, at, size), block(near, at, size),
+            core_send.at[at], core_recv.at[at], other,
+        )
+
+    def copy1(step, cut):
+        part, delta = split_step(step)
+        at, size = step * PIECES + cut, 16 * PART // PIECES
+        return send(
+            block(home, at, size), block(land1, at, size),
+            s1.at[at], r1.at[at], peer(part, 0, delta),
         )
 
     def part_copy(source, target, count, sends, recvs, level, step):
@@ -221,7 +238,6 @@
             sends.at[step], recvs.at[step], peer(part, level, delta),
         )
 
-    copy1 = functools.partial(part_copy, home, land1, 16 * PART, s1, r1, 0)
     copy2 = functools.partial(part_copy, sum1, land2, 4 * PART, s2, r2, 1)
     copy3 = functools.partial(part_copy, sum2, land3, PART, s3, r3, 2)
     core_sign = 1.0 - 2.0 * core.astype(jnp.float32)
@@ -234,78 +250,75 @@
 
     pl.semaphore_wait(barrier, 10)
 
-    for at in range(12 + AHEAD):
-        if at < 12:
-            gather(at, 1 - core, write_away)
-            core_copy(at).start()
+    order = [(hop * 3 + part, cut) for cut in range(PIECES) for hop in range(3) for part in range(3)]
+    order += [(9 + part, cut) for part in range(3) for cut in range(PIECES)]
+    for at in range(len(order) + AHEAD):
+        if at < len(order):
+            gather(*order[at], 1 - core, write_away)
+            core_copy(*order[at]).start()
         if at >= AHEAD:
-            step = at - AHEAD
-            core_copy(step).wait_recv()
-            gather(step, core, write_home)
+            step, cut = order[at - AHEAD]
+            core_copy(step, cut).wait_recv()
+            gather(step, cut, core, write_home)
             if step < 9:
-                copy1(step).start()
+                copy1(step, cut).start()
 
     def total(own, landed, part, level, own_at, land_at, land_stride):
         out = sign(part, level, 0) * own[pl.ds(own_at, 8), :]
         for hop in range(3):
             delta = (DELTAS >> (2 * hop)) & 3
-            at = pl.multiple_of(land_at + hop * land_stride, 8)
+            at = land_at + hop * land_stride
             out = out + sign(part, level, delta) * landed[pl.ds(at, 8), :]
         return out
 
     def fold(own, landed, count, level, copy_in, target, copy_out):
         whole = 4 * count
 
-        def one(step, carry):
+        for part in range(3):
+            for hop in range(3):
+                copy_in(hop * 3 + part)
+        for step in range(12):
             part, delta = split_step(step)
 
-            @pl.when(step < 3)
-            def _():
-                for hop in range(3):
-                    copy_in(hop * 3 + part).wait_recv()
-
-            def tile(t, carry):
+            for t in range(count // 8):
                 inside = delta * count + t * 8
-                target[pl.ds(pl.multiple_of(step * count + t * 8, 8), 8), :] = total(
+                target[pl.ds(step * count + t * 8, 8), :] = total(
                     own, landed, part, level,
-                    pl.multiple_of((9 + part) * whole + inside, 8), part * whole + inside, 3 * whole,
+                    (9 + part) * whole + inside, part * whole + inside, 3 * whole,
                 )
-                return carry
-
-            lax.fori_loop(0, count // 8, tile, 0, unroll=3)
-
-            @pl.when(step < 9)
-            def _():
+            if step < 9:
                 copy_out(step).start()
 
-            return carry
-
-        lax.fori_loop(0, 12, one, 0)
-
-    fold(home, land1, 4 * PART, 0, copy1, sum1, copy2)
-    fold(sum1, land2, PART, 1, copy2, sum2, copy3)
-
-    def finish(part, carry):
+    def landed1(step):
+        for cut in range(PIECES):
+            copy1(step, cut).wait_recv()
+
+    fold(home, land1, 4 * PART, 0, landed1, sum1, copy2)
+    fold(sum1, land2, PART, 1, lambda step: copy2(step).wait_recv(), sum2, copy3)
+
+    for part in range(3):
         for hop in range(3):
             copy3(hop * 3 + part).wait_recv()
         for t in range(PART // 8):
             inside = part * PART + t * 8
-            sketch[pl.ds(pl.multiple_of(inside, 8), 8), :] = scale * total(
-                sum2, land3, part, 2, pl.multiple_of(9 * PART + inside, 8), inside, 3 * PART
+            sketch[pl.ds(inside, 8), :] = scale * total(
+                sum2, land3, part, 2, 9 * PART + inside, inside, 3 * PART
             )
-        return carry
-
-    lax.fori_loop(0, 3, finish, 0)
 
     rows_here = jnp.concatenate(
         [sketch[:samples, :], jnp.zeros((COLS - samples, COLS), jnp.float32)], axis=0
     )
     turned = jnp.transpose(rows_here)
     device_total = lax.axis_size("hi") * lax.axis_size("lo")
-    gram[0, :COLS, :] = jnp.dot(
+    local = jnp.dot(
         turned, rows_here, precision=lax.Precision.HIGHEST, preferred_element_type=jnp.float32
     ) * (1.0 / (samples * device_total))
-    gram[0, COLS:, :] = jnp.zeros((3 * GRAM_PART - COLS, COLS), jnp.float32)
+    half, quarter = COLS // 2, COLS // 4
+    left_half = lax.broadcasted_iota(jnp.int32, (quarter, COLS), 1) < half
+    gram[0, :half, :] = local[:half]
+    gram[0, half:, :] = jnp.where(
+        left_half, pltpu.roll(local[half : half + quarter], half, 1), local[half + quarter :]
+    )
 
     core_gram = send(gram.at[0], core_land, gcs, gcr, other)
     core_gram.start()
@@ -314,56 +327,46 @@
 
     def gram_copy(stage, step):
         part, delta = split_step(step)
-        span = pl.ds(pl.multiple_of(part * GRAM_PART, 8), GRAM_PART)
         at = stage * 9 + step
         return send(
-            gram.at[stage + 1, span], gram_land.at[stage * 3 + step // 3, span],
+            block(gram.at[stage + 1], part, GRAM_PART),
+            block(gram_land.at[stage * 3 + step // 3], part, GRAM_PART),
             gs.at[at], gr.at[at], peer(part, stage, delta),
         )
 
-    def gram_stage(stage, carry):
-        def start(step, carry):
+    for stage in range(3):
+        for step in range(9):
             gram_copy(stage, step).start()
-            return carry
-
-        lax.fori_loop(0, 9, start, 0)
-
-        def add(part, carry):
+        for part in range(3):
             for hop in range(3):
                 gram_copy(stage, hop * 3 + part).wait_recv()
-            for t in range(GRAM_PART // 8):
-                span = pl.ds(pl.multiple_of(part * GRAM_PART + t * 8, 8), 8)
-                own = gram[stage + 1, span, :]
-                two, one, three = (gram_land[stage * 3 + hop, span, :] for hop in range(3))
-                gram[stage + 2, span, :] = (own + two) + (one + three)
-            return carry
-
-        return lax.fori_loop(0, 3, add, carry)
-
-    lax.fori_loop(0, 3, gram_stage, 0)
+            span = pl.ds(part * GRAM_PART, GRAM_PART)
+            own = gram[stage + 1, span, :]
+            two, one, three = (gram_land[stage * 3 + hop, span, :] for hop in range(3))
+            gram[stage + 2, span, :] = (own + two) + (one + three)
 
     def put(base, value):
         augmented[base : base + BLOCK, :] = value
 
-    eliminate(jnp.concatenate([gram[4, :COLS, :], turned], axis=1), put)
+    packed = gram[4, half:, :]
+    whole_gram = jnp.concatenate(
+        [gram[4, :half, :], pltpu.roll(packed, half, 1), packed], axis=0
+    )
+    eliminate(jnp.concatenate([whole_gram, turned], axis=1), put)
     row_at = lax.broadcasted_iota(jnp.int32, (COLS, COLS), 0)
     col_at = lax.broadcasted_iota(jnp.int32, (COLS, COLS), 1)
     r_ref[...] = jnp.where(row_at <= col_at, augmented[:, :COLS], 0.0)
     q_ref[...] = jnp.transpose(augmented[:, COLS:])[:samples, :]
 
-    def drain_core(step, carry):
-        core_copy(step).wait_send()
-        return carry
-
-    def drain(step, carry):
-        for copy in (copy1, copy2, copy3):
+    for step, cut in order:
+        core_copy(step, cut).wait_send()
+        if step < 9:
+            copy1(step, cut).wait_send()
+    for step in range(9):
+        for copy in (copy2, copy3):
             copy(step).wait_send()
         for stage in range(3):
             gram_copy(stage, step).wait_send()
-        return carry
-
-    lax.fori_loop(0, 12, drain_core, 0)
-    lax.fori_loop(0, 9, drain, 0)
     core_gram.wait_send()
 
 
@@ -401,8 +404,8 @@
             pltpu.VMEM((9, 3 * GRAM_PART, cols), f32),
             pltpu.VMEM((3 * GRAM_PART, cols), f32),
             pltpu.VMEM((cols, 2 * cols), f32),
-            dma((LOADS,)), dma, dma, dma((12,)), dma((12,)),
-            dma((9,)), dma((9,)), dma((9,)), dma((9,)), dma((9,)), dma((9,)),
+            dma((LOADS,)), dma, dma, dma((12 * PIECES,)), dma((12 * PIECES,)),
+            dma((9 * PIECES,)), dma((9 * PIECES,)), dma((9,)), dma((9,)), dma((9,)), dma((9,)),
             dma((27,)), dma((27,)), dma, dma,
         ],
         compiler_params=pltpu.CompilerParams(

time: 57.5 us -> 54 us (0.939)
  Pallas kernels: 55.2 us -> 52 us
    pallas_call x1, Pallas kernels: 55.2 us -> 52 us  [shards(): pl.pallas_call(functools.partial(kernel, 1.0 / math.sqrt(rows * devices),...]
where the time goes in v4:
time: 54 us; the launch traced here: 53.9 us
  Pallas kernels  52 us (96%)
  local copies, waits for them, and re-layouts  1.25 us (2%)
  between operations  0.64 us (1%)
    pallas_call x1, Pallas kernels, shards(): pl.pallas_call(functools.partial(kernel, 1.0 / math.sqrt(rows * devices),...  52 us
    unnamed x2, local copies, waits for them, and re-layouts  1.25 us

profile of v4, /device:TPU:0, one launch (start us, length us, event | category | flops | bytes accessed | tf_op | source)
XLA Modules:
  0.0 53.9 jit_solution(11149334668038886651)
XLA Ops:
  0.6 52.0 %sketch_qr.1 = (f32[64,128]{1,0:T(8,128)S(1)}, f32[128,128]{1,0:T(8,128)S(1)}) custom-call(f32[16384,128]{1,0:T(8,128)} %panel_hbm.1, s32[128,128]{1,0:T(8,128)} %bitcast.1, s32[8192]{0:T(1024)} %index_hbm.1), custom_call_target="tpu_custom_call" | custom-call | tf_op jit(solution)/shard_map/sketch_qr/pallas_call | solution.py:385
  52.7 0.6 %copy.7 = f32[64,128]{1,0:T(8,128)} copy(f32[64,128]{1,0:T(8,128)S(1)} %get-tuple-element.2) | data formatting | bytes 65536
  53.3 0.6 %copy.8 = f32[128,128]{1,0:T(8,128)} copy(f32[128,128]{1,0:T(8,128)S(1)} %get-tuple-element.3) | data formatting | bytes 131072

commit v5 on v4

--- a/solution.py
+++ b/solution.py
@@ -15,10 +15,10 @@
 BLOCK = 16
 PART = 24
 GRAM_PART = 32
+GATHER_UNROLL = 1
 IN_FLIGHT = 4
-PIECES = 2
 DELTAS = 0x36
-AHEAD = 3
+AHEAD = 6
 
 
 def parity_sign(value, bits):
@@ -197,18 +197,19 @@
         part, delta = split_step(step)
         count = min(PART, samples - part * PART)
 
-        def one(j, carry):
-            for inner in range(4):
-                to_chip = chip ^ (
-                    (delta << shift(part, 0)) | (j << shift(part, 1)) | (inner << shift(part, 2))
-                )
-                base = (to_chip * 2 + which) * samples + part * PART
-                to = pl.multiple_of(step * 16 * PART + (j * 4 + inner) * PART, 8)
-                for k in range(count):
-                    write(to + k, work[pl.ds(index[base + k], 1), :])
+        second = (DELTAS >> (2 * cut)) & 3
+
+        def one(third, carry):
+            to_chip = chip ^ (
+                (delta << shift(part, 0)) | (second << shift(part, 1)) | (third << shift(part, 2))
+            )
+            base = (to_chip * 2 + which) * samples + part * PART
+            to = pl.multiple_of(step * 16 * PART + (second * 4 + third) * PART, 8)
+            for k in range(count):
+                write(to + k, work[pl.ds(index[base + k], 1), :])
             return carry
 
-        lax.fori_loop(cut * 4 // PIECES, (cut + 1) * 4 // PIECES, one, 0)
+        lax.fori_loop(0, 4, one, 0, unroll=GATHER_UNROLL)
 
     def send(source, target, send_sem, recv_sem, to):
         return pltpu.make_async_remote_copy(
@@ -217,7 +218,7 @@
         )
 
     def core_copy(step, cut):
-        at, size = step * PIECES + cut, 16 * PART // PIECES
+        at, size = step * 4 + ((DELTAS >> (2 * cut)) & 3), 4 * PART
         return send(
             block(away, at, size), block(near, at, size),
             core_send.at[at], core_recv.at[at], other,
@@ -225,7 +226,7 @@
 
     def copy1(step, cut):
         part, delta = split_step(step)
-        at, size = step * PIECES + cut, 16 * PART // PIECES
+        at, size = step * 4 + ((DELTAS >> (2 * cut)) & 3), 4 * PART
         return send(
             block(home, at, size), block(land1, at, size),
             s1.at[at], r1.at[at], peer(part, 0, delta),
@@ -250,8 +251,8 @@
 
     pl.semaphore_wait(barrier, 10)
 
-    order = [(hop * 3 + part, cut) for cut in range(PIECES) for hop in range(3) for part in range(3)]
-    order += [(9 + part, cut) for part in range(3) for cut in range(PIECES)]
+    order = [(hop * 3 + part, cut) for cut in range(4) for hop in range(3) for part in range(3)]
+    order += [(9 + part, cut) for part in range(3) for cut in range(4)]
     for at in range(len(order) + AHEAD):
         if at < len(order):
             gather(*order[at], 1 - core, write_away)
@@ -274,11 +275,10 @@
     def fold(own, landed, count, level, copy_in, target, copy_out):
         whole = 4 * count
 
-        for part in range(3):
-            for hop in range(3):
-                copy_in(hop * 3 + part)
         for step in range(12):
             part, delta = split_step(step)
+            for hop in range(3):
+                copy_in(hop * 3 + part, step // 3)
 
             for t in range(count // 8):
                 inside = delta * count + t * 8
@@ -289,12 +289,15 @@
             if step < 9:
                 copy_out(step).start()
 
-    def landed1(step):
-        for cut in range(PIECES):
-            copy1(step, cut).wait_recv()
+    def landed1(step, cut):
+        copy1(step, cut).wait_recv()
+
+    def landed2(step, cut):
+        if cut == 0:
+            copy2(step).wait_recv()
 
     fold(home, land1, 4 * PART, 0, landed1, sum1, copy2)
-    fold(sum1, land2, PART, 1, lambda step: copy2(step).wait_recv(), sum2, copy3)
+    fold(sum1, land2, PART, 1, landed2, sum2, copy3)
 
     for part in range(3):
         for hop in range(3):
@@ -404,8 +407,8 @@
             pltpu.VMEM((9, 3 * GRAM_PART, cols), f32),
             pltpu.VMEM((3 * GRAM_PART, cols), f32),
             pltpu.VMEM((cols, 2 * cols), f32),
-            dma((LOADS,)), dma, dma, dma((12 * PIECES,)), dma((12 * PIECES,)),
-            dma((9 * PIECES,)), dma((9 * PIECES,)), dma((9,)), dma((9,)), dma((9,)), dma((9,)),
+            dma((LOADS,)), dma, dma, dma((48,)), dma((48,)),
+            dma((36,)), dma((36,)), dma((9,)), dma((9,)), dma((9,)), dma((9,)),
             dma((27,)), dma((27,)), dma, dma,
         ],
         compiler_params=pltpu.CompilerParams(

time: 54 us -> 52.3 us (0.969)
  Pallas kernels: 52 us -> 50.3 us
    pallas_call x1, Pallas kernels: 52 us -> 50.3 us  [shards(): pl.pallas_call(functools.partial(kernel, 1.0 / math.sqrt(rows * devices),...]
where the time goes in v5:
time: 52.3 us; the launch traced here: 52.2 us
  Pallas kernels  50.3 us (96%)
  local copies, waits for them, and re-layouts  1.25 us (2%)
  between operations  0.64 us (1%)
    pallas_call x1, Pallas kernels, shards(): pl.pallas_call(functools.partial(kernel, 1.0 / math.sqrt(rows * devices),...  50.3 us
    unnamed x2, local copies, waits for them, and re-layouts  1.25 us

profile of v5, /device:TPU:0, one launch (start us, length us, event | category | flops | bytes accessed | tf_op | source)
XLA Modules:
  0.0 52.2 jit_solution(14328537362221076396)
XLA Ops:
  0.6 50.3 %sketch_qr.1 = (f32[64,128]{1,0:T(8,128)S(1)}, f32[128,128]{1,0:T(8,128)S(1)}) custom-call(f32[16384,128]{1,0:T(8,128)} %panel_hbm.1, s32[128,128]{1,0:T(8,128)} %bitcast.1, s32[8192]{0:T(1024)} %index_hbm.1), custom_call_target="tpu_custom_call" | custom-call | tf_op jit(solution)/shard_map/sketch_qr/pallas_call | solution.py:388
  50.9 0.6 %copy.7 = f32[64,128]{1,0:T(8,128)} copy(f32[64,128]{1,0:T(8,128)S(1)} %get-tuple-element.2) | data formatting | bytes 65536
  51.5 0.6 %copy.8 = f32[128,128]{1,0:T(8,128)} copy(f32[128,128]{1,0:T(8,128)S(1)} %get-tuple-element.3) | data formatting | bytes 131072

commit v6 on v5

--- a/solution.py
+++ b/solution.py
@@ -189,8 +189,8 @@
 
         lax.fori_loop(0, outer // order, group, 0)
 
-    butterflies(per_load, per_load * MIX, MIX, 2)
-    butterflies(LOADS, MIX, per_load * MIX, 4)
+    butterflies(per_load, per_load * MIX, MIX, 4)
+    butterflies(LOADS, MIX, per_load * MIX, 8)
     index_move.wait()
 
     def gather(step, cut, which, write):
@@ -337,9 +337,17 @@
             gs.at[at], gr.at[at], peer(part, stage, delta),
         )
 
+    for step in range(9):
+        gram_copy(0, step).start()
+    for step, cut in order:
+        core_copy(step, cut).wait_send()
+        if step < 9:
+            copy1(step, cut).wait_send()
+    for step in range(9):
+        for copy in (copy2, copy3):
+            copy(step).wait_send()
+    core_gram.wait_send()
     for stage in range(3):
-        for step in range(9):
-            gram_copy(stage, step).start()
         for part in range(3):
             for hop in range(3):
                 gram_copy(stage, hop * 3 + part).wait_recv()
@@ -347,6 +355,11 @@
             own = gram[stage + 1, span, :]
             two, one, three = (gram_land[stage * 3 + hop, span, :] for hop in range(3))
             gram[stage + 2, span, :] = (own + two) + (one + three)
+            if stage < 2:
+                for hop in range(3):
+                    gram_copy(stage + 1, hop * 3 + part).start()
+        for step in range(9):
+            gram_copy(stage, step).wait_send()
 
     def put(base, value):
         augmented[base : base + BLOCK, :] = value
@@ -360,17 +373,6 @@
     col_at = lax.broadcasted_iota(jnp.int32, (COLS, COLS), 1)
     r_ref[...] = jnp.where(row_at <= col_at, augmented[:, :COLS], 0.0)
     q_ref[...] = jnp.transpose(augmented[:, COLS:])[:samples, :]
-
-    for step, cut in order:
-        core_copy(step, cut).wait_send()
-        if step < 9:
-            copy1(step, cut).wait_send()
-    for step in range(9):
-        for copy in (copy2, copy3):
-            copy(step).wait_send()
-        for stage in range(3):
-            gram_copy(stage, step).wait_send()
-    core_gram.wait_send()
 
 
 def shards(panel, signs, sample_rows):

time: 52.3 us -> 51.5 us (0.985)
  Pallas kernels: 50.3 us -> 49.5 us
    pallas_call x1, Pallas kernels: 50.3 us -> 49.5 us  [shards(): pl.pallas_call(functools.partial(kernel, 1.0 / math.sqrt(rows * devices),...]
where the time goes in v6:
time: 51.5 us; the launch traced here: 51.4 us
  Pallas kernels  49.5 us (96%)
  local copies, waits for them, and re-layouts  1.25 us (2%)
  between operations  0.64 us (1%)
    pallas_call x1, Pallas kernels, shards(): pl.pallas_call(functools.partial(kernel, 1.0 / math.sqrt(rows * devices),...  49.5 us
    unnamed x2, local copies, waits for them, and re-layouts  1.25 us

profile of v6, /device:TPU:0, one launch (start us, length us, event | category | flops | bytes accessed | tf_op | source)
XLA Modules:
  0.0 51.4 jit_solution(5334091463924074050)
XLA Ops:
  0.6 49.5 %sketch_qr.1 = (f32[64,128]{1,0:T(8,128)S(1)}, f32[128,128]{1,0:T(8,128)S(1)}) custom-call(f32[16384,128]{1,0:T(8,128)} %panel_hbm.1, s32[128,128]{1,0:T(8,128)} %bitcast.1, s32[8192]{0:T(1024)} %index_hbm.1), custom_call_target="tpu_custom_call" | custom-call | tf_op jit(solution)/shard_map/sketch_qr/pallas_call | solution.py:390
  50.2 0.6 %copy.7 = f32[64,128]{1,0:T(8,128)} copy(f32[64,128]{1,0:T(8,128)S(1)} %get-tuple-element.2) | data formatting | bytes 65536
  50.8 0.6 %copy.8 = f32[128,128]{1,0:T(8,128)} copy(f32[128,128]{1,0:T(8,128)S(1)} %get-tuple-element.3) | data formatting | bytes 131072

commit v7 on v6

--- a/solution.py
+++ b/solution.py
@@ -119,18 +119,6 @@
     def block(ref, at, count):
         return ref.at[pl.ds(at * count if isinstance(at, int) else pl.multiple_of(at * count, 8), count)]
 
-    other = device(chip, 1 - core)
-    barrier = pltpu.get_barrier_semaphore()
-    pl.semaphore_signal(barrier, inc=1, device_id=other, device_id_type=MESH)
-
-    def greet(step, carry):
-        pl.semaphore_signal(
-            barrier, inc=1, device_id=peer(step % 3, 0, step // 3 + 1), device_id_type=MESH
-        )
-        return carry
-
-    lax.fori_loop(0, 9, greet, 0)
-
     outer = rows // MIX
     per_load = outer // LOADS
     piece = rows // LOADS
@@ -145,6 +133,16 @@
         load(at).start()
     index_copy = pltpu.make_async_copy(index_hbm, index_rows, index_sem)
     index_copy.start()
+    other = device(chip, 1 - core)
+    barrier = pltpu.get_barrier_semaphore()
+    pl.semaphore_signal(barrier, inc=1, device_id=other, device_id_type=MESH)
+
+    for part in range(3):
+        for delta in range(1, 4):
+            pl.semaphore_signal(
+                barrier, inc=1, device_id=peer(part, 0, delta), device_id_type=MESH
+            )
+
     mix[...] = hadamard(MIX).astype(jnp.bfloat16)
     sign_copy.wait()
 

time: 51.5 us -> 51.1 us (level)
  no operation moved by 1% of the time
where the time goes in v7:
time: 51.1 us; the launch traced here: 51 us
  Pallas kernels  49.1 us (96%)
  local copies, waits for them, and re-layouts  1.25 us (2%)
  between operations  0.64 us (1%)
    pallas_call x1, Pallas kernels, shards(): pl.pallas_call(functools.partial(kernel, 1.0 / math.sqrt(rows * devices),...  49.1 us
    unnamed x2, local copies, waits for them, and re-layouts  1.25 us

profile of v7, /device:TPU:0, one launch (start us, length us, event | category | flops | bytes accessed | tf_op | source)
XLA Modules:
  0.0 51.0 jit_solution(7706151832275140559)
XLA Ops:
  0.6 49.1 %sketch_qr.1 = (f32[64,128]{1,0:T(8,128)S(1)}, f32[128,128]{1,0:T(8,128)S(1)}) custom-call(f32[16384,128]{1,0:T(8,128)} %panel_hbm.1, s32[128,128]{1,0:T(8,128)} %bitcast.1, s32[8192]{0:T(1024)} %index_hbm.1), custom_call_target="tpu_custom_call" | custom-call | tf_op jit(solution)/shard_map/sketch_qr/pallas_call | solution.py:388
  49.8 0.6 %copy.7 = f32[64,128]{1,0:T(8,128)} copy(f32[64,128]{1,0:T(8,128)S(1)} %get-tuple-element.2) | data formatting | bytes 65536
  50.4 0.6 %copy.8 = f32[128,128]{1,0:T(8,128)} copy(f32[128,128]{1,0:T(8,128)S(1)} %get-tuple-element.3) | data formatting | bytes 131072
